TPU v7x, 32 devices: a whole 2x2x4 slice. The times are simulated.
32 devices in a mesh: parts: 1, rows: 8 (over z, y), branch: 2 (over core), head: 2 (over x).
Axes of the slice: x: 2, y: 2, z: 4, core: 2. Of those that a mesh axis runs over, the one named last changes fastest.
Arguments:
- lineup_state: bfloat16 [32, 128, 256], P(('parts', 'rows', 'branch')), may hold values from -12 to 12
- pairwise: bfloat16 [128, 128, 128], P(('parts', 'rows', 'branch')), may hold values from -12 to 12
- aligned_residue_bounds: int32 [32, 2], P('parts'), may hold values from 0 to 128, as said below
- residue_valid_mask: int32 [128], P('parts'), may hold values from 0 to 1, as said below
- coupling_offset_weight_map: bfloat16 [128, 8], P(None, 'head'), may hold values from -0.5 to 0.5
- triangle_bias_matrix: bfloat16 [128, 4], P(None, 'head'), may hold values from -0.5 to 0.5
- alignment_projection_matrix: bfloat16 [4, 256, 256], P(None, None, 'head'), may hold values from -1 to 1
- lineup_readout_weight: bfloat16 [256, 256], replicated, may hold values from -4 to 4
- feedfwd_entry_weight: bfloat16 [256, 1024], P(None, 'head'), may hold values from -0.375 to 0.375
- feedfwd_exit_weight: bfloat16 [1024, 256], P('head'), may hold values from -0.1875 to 0.1875
- pair_projection_matrix: bfloat16 [4, 128, 128], P(None, None, 'head'), may hold values from -2 to 2
- pair_output_matrix: bfloat16 [128, 128], P(None, 'head'), may hold values from -6 to 6
- left_right_maps: bfloat16 [2, 256, 32], replicated, may hold values from -0.375 to 0.375
- outer_product_output_matrix: bfloat16 [1024, 128], P(None, 'head'), may hold values from -1.5 to 1.5
Outputs:
- refreshed_lineup_state: bfloat16 [32, 128, 256], P(('parts', 'rows', 'branch'), None, 'head')
- pairwise_out: bfloat16 [128, 128, 128], P(('parts', 'rows', 'branch'), None, 'head')
Inputs may be any that keep to these rules, and one draw needn't show every extreme that they name: `aligned_residue_bounds`: each row holds a start below its end; row 0 covers all 128 residues; every span covers a quarter of the 128 residues or more and starts in the first half. `residue_valid_mask`: 1 on a prefix that holds at least half of the 128 residues, 0 after it; the last residue is always 0.
All inputs are finite; a program needn't handle non-finite values.
Results may differ from a plain program's by a relative error of at most 0.011.
Values may be sent and summed in bfloat16 or wider, within the bound.
A program may use at most 64 MiB of HBM per device.

v0:
```python
import math

import jax
import jax.numpy as jnp
from jax import lax
from jax.sharding import PartitionSpec as P

PER_FOCUS_DIM = 32


def layer_normalize(values):
    values = values.astype(jnp.float32)
    center = values - jnp.mean(values, -1, keepdims=True)
    spread = jnp.mean(center * center, -1, keepdims=True)
    return center * lax.rsqrt(spread + 1e-05)


def soft_weights(attention_scores):
    row_max = jnp.max(attention_scores, -1, keepdims=True)
    shifted = jnp.exp(attention_scores - row_max)
    return (shifted / jnp.sum(shifted, -1, keepdims=True)).astype(jnp.bfloat16)


def span_mask(aligned_residue_bounds, length_value):
    places = jnp.arange(length_value, dtype=jnp.int32)
    inside = (places[None, :] >= aligned_residue_bounds[:, 0:1]) & (
        places[None, :] < aligned_residue_bounds[:, 1:2]
    )
    return inside.astype(jnp.float32)


def local(
    lineup_state,
    pairwise,
    aligned_residue_bounds,
    residue_valid_mask,
    coupling_offset_weight_map,
    triangle_bias_matrix,
    alignment_projection_matrix,
    lineup_readout_weight,
    feedfwd_entry_weight,
    feedfwd_exit_weight,
    pair_projection_matrix,
    pair_output_matrix,
    left_right_maps,
    outer_product_output_matrix,
):
    sequence_shard_count = lineup_state.shape[0]
    length_value = lineup_state.shape[1]
    residue_shard_count = pairwise.shape[0]
    alignment_heads_sharded = coupling_offset_weight_map.shape[1]
    pairwise_heads_sharded = triangle_bias_matrix.shape[1]
    inv_scale = 1.0 / math.sqrt(PER_FOCUS_DIM)
    row_place = lax.axis_index(("rows", "branch"))
    head_location = lax.axis_index("head")
    seq_start = row_place * sequence_shard_count
    row_start = row_place * residue_shard_count
    mask_full = span_mask(aligned_residue_bounds, length_value)
    mask_own = lax.dynamic_slice_in_dim(mask_full, seq_start, sequence_shard_count, 0)
    key_valid = residue_valid_mask > 0
    alignment_normed = layer_normalize(lineup_state).astype(jnp.bfloat16)
    pair_normed = layer_normalize(pairwise).astype(jnp.bfloat16)
    bias_matrix = jnp.concatenate([coupling_offset_weight_map, triangle_bias_matrix], axis=1)
    bias_local = jnp.einsum(
        "tue,el->ltu", pair_normed, bias_matrix, preferred_element_type=jnp.float32
    ).astype(jnp.bfloat16)
    lineup_mapped = jnp.einsum(
        "tvf,xfp->xtvp",
        alignment_normed,
        alignment_projection_matrix,
        preferred_element_type=jnp.float32,
    )
    lineup_probe_lookup_content = (
        lineup_mapped[:3]
        .astype(jnp.bfloat16)
        .reshape(3, sequence_shard_count, length_value, alignment_heads_sharded, PER_FOCUS_DIM)
    )
    alignment_gate = jax.nn.sigmoid(lineup_mapped[3])
    pair_proj = jnp.einsum(
        "ijc,gcd->gijd", pair_normed, pair_projection_matrix, preferred_element_type=jnp.float32
    )
    pair_qkv = (
        pair_proj[:3]
        .astype(jnp.bfloat16)
        .reshape(3, residue_shard_count, length_value, pairwise_heads_sharded, PER_FOCUS_DIM)
    )
    pair_gate = jax.nn.sigmoid(pair_proj[3])
    bias_portion = lax.all_gather(bias_local, ("rows", "branch"), axis=1, tiled=True)
    row_total_count = bias_portion.shape[1]
    alignment_query = lineup_probe_lookup_content[0]
    attention_scores = (
        jnp.einsum(
            "xtza,xfza->xztf",
            alignment_query,
            lineup_probe_lookup_content[1],
            preferred_element_type=jnp.float32,
        )
        * inv_scale
    )
    attention_scores = (
        attention_scores + bias_portion[:alignment_heads_sharded].astype(jnp.float32)[None]
    )
    attention_scores = jnp.where(mask_own[:, None, None, :] > 0, attention_scores, -1000000000.0)
    softmax_shares = soft_weights(attention_scores)
    alignment_portion = jnp.einsum(
        "fxkc,fcxz->fkxz",
        softmax_shares,
        lineup_probe_lookup_content[2],
        preferred_element_type=jnp.float32,
    )
    alignment_portion = alignment_portion.reshape(
        sequence_shard_count, row_total_count, alignment_heads_sharded * PER_FOCUS_DIM
    )
    alignment_portion = (alignment_portion * alignment_gate).astype(jnp.bfloat16)
    pair_query = pair_qkv[0]
    triangle_scores = (
        jnp.einsum("ijhd,ikhd->ihjk", pair_query, pair_qkv[1], preferred_element_type=jnp.float32)
        * inv_scale
    )
    triangle_scores = (
        triangle_scores + bias_portion[alignment_heads_sharded:].astype(jnp.float32)[None]
    )
    triangle_scores = jnp.where(key_valid[None, None, None, :], triangle_scores, -1000000000.0)
    tri_weights = soft_weights(triangle_scores)
    pair_part = jnp.einsum(
        "ihjk,ikhd->ijhd", tri_weights, pair_qkv[2], preferred_element_type=jnp.float32
    )
    pair_part = pair_part.reshape(
        residue_shard_count, row_total_count, pairwise_heads_sharded * PER_FOCUS_DIM
    )
    pair_part = (pair_part * pair_gate).astype(jnp.bfloat16)
    alignment_flattened = jnp.transpose(alignment_portion, (1, 0, 2)).reshape(
        row_total_count, sequence_shard_count * alignment_heads_sharded * PER_FOCUS_DIM
    )
    pair_flattened = jnp.transpose(pair_part, (1, 0, 2)).reshape(
        row_total_count, residue_shard_count * pairwise_heads_sharded * PER_FOCUS_DIM
    )
    attention_result = jnp.concatenate([alignment_flattened, pair_flattened], axis=1)
    alignment_width = sequence_shard_count * alignment_heads_sharded * PER_FOCUS_DIM
    alignment_local = jnp.transpose(
        attention_result[:, :alignment_width].reshape(
            length_value, sequence_shard_count, alignment_heads_sharded * PER_FOCUS_DIM
        ),
        (1, 0, 2),
    )
    pair_local = jnp.transpose(
        attention_result[:, alignment_width:].reshape(
            length_value, residue_shard_count, pairwise_heads_sharded * PER_FOCUS_DIM
        ),
        (1, 0, 2),
    )
    lineup_focus_split, pairwise_heads = (
        lax.all_gather(alignment_local, "head", axis=2, tiled=True),
        lax.all_gather(pair_local, "head", axis=2, tiled=True),
    )
    outer_factors = jnp.einsum(
        "juf,bfn->bjun", alignment_normed, left_right_maps, preferred_element_type=jnp.float32
    )
    outer_factors = (outer_factors * mask_own[None, :, :, None]).astype(jnp.bfloat16)
    factor_rows = lax.all_to_all(
        outer_factors[0], ("rows", "branch"), split_axis=1, concat_axis=0, tiled=True
    )
    col_factors = lax.all_gather(outer_factors[1], ("rows", "branch"), axis=0, tiled=True)
    mask_rows = lax.dynamic_slice_in_dim(mask_full, row_start, residue_shard_count, 1)
    pair_count = jnp.dot(mask_rows.T, mask_full, precision=lax.Precision.HIGHEST)
    col_block = math.gcd(length_value, 128)

    def outer_block(col_start):
        block_cols = lax.dynamic_slice_in_dim(col_factors, col_start, col_block, 1)
        outer_sum = lax.dot_general(
            factor_rows, block_cols, (((0,), (0,)), ((), ())), preferred_element_type=jnp.float32
        )
        counts = lax.dynamic_slice_in_dim(pair_count, col_start, col_block, 1)
        outer_mean = (outer_sum / counts[:, None, :, None]).astype(jnp.bfloat16)
        outer_mean = jnp.transpose(outer_mean, (0, 2, 1, 3)).reshape(
            residue_shard_count * col_block, -1
        )
        return jnp.dot(
            outer_mean, outer_product_output_matrix, preferred_element_type=jnp.float32
        ).reshape(residue_shard_count, col_block, -1)

    starts = jnp.arange(length_value // col_block, dtype=jnp.int32) * col_block
    opm_blocks = lax.map(outer_block, starts)
    opm_update = jnp.transpose(opm_blocks, (1, 0, 2, 3)).reshape(
        residue_shard_count, length_value, -1
    )
    width_z = pair_output_matrix.shape[1]
    tri_update = jnp.dot(
        pairwise_heads.reshape(residue_shard_count * length_value, -1),
        pair_output_matrix,
        preferred_element_type=jnp.float32,
    ).reshape(residue_shard_count, length_value, width_z)
    pair_own = lax.dynamic_slice_in_dim(pairwise, head_location * width_z, width_z, 2).astype(
        jnp.float32
    )
    pairwise_out = (pair_own + tri_update + opm_update).astype(jnp.bfloat16)
    channels = lineup_state.shape[2]
    lineup_blended = lineup_state.astype(jnp.float32) + jnp.dot(
        lineup_focus_split.reshape(sequence_shard_count * length_value, -1),
        lineup_readout_weight,
        preferred_element_type=jnp.float32,
    ).reshape(sequence_shard_count, length_value, channels)
    feedfwd_standardized = layer_normalize(lineup_blended).astype(jnp.bfloat16)
    head_count = lax.axis_size("head")
    hidden = jax.nn.relu(
        jnp.einsum(
            "src,cf->srf",
            feedfwd_standardized,
            feedfwd_entry_weight,
            preferred_element_type=jnp.float32,
        )
    ).astype(jnp.bfloat16)
    partial_value = jnp.einsum(
        "srf,fc->src", hidden, feedfwd_exit_weight, preferred_element_type=jnp.float32
    )
    summed_result = lax.psum_scatter(
        partial_value.astype(jnp.bfloat16), "head", scatter_dimension=2, tiled=True
    ).astype(jnp.float32)
    alignment_channel_width = channels // head_count
    alignment_owned = lax.dynamic_slice_in_dim(
        lineup_blended, head_location * alignment_channel_width, alignment_channel_width, 2
    )
    refreshed_lineup_state = (alignment_owned + summed_result).astype(jnp.bfloat16)
    return (refreshed_lineup_state, pairwise_out)


def solution(mesh):
    in_specs = (
        P(("parts", "rows", "branch"), None, None),
        P(("parts", "rows", "branch"), None, None),
        P("parts", None),
        P("parts"),
        P(None, "head"),
        P(None, "head"),
        P(None, None, "head"),
        P(),
        P(None, "head"),
        P("head", None),
        P(None, None, "head"),
        P(None, "head"),
        P(),
        P(None, "head"),
    )
    out_specs = (
        P(("parts", "rows", "branch"), None, "head"),
        P(("parts", "rows", "branch"), None, "head"),
    )
    return jax.shard_map(local, mesh=mesh, in_specs=in_specs, out_specs=out_specs, check_vma=False)
```

profile of v0, /device:TPU:0, one launch (start us, length us, event | category | flops | bytes accessed | tf_op | source)
XLA Modules:
  0.0 93.4 jit_solution(9554350493809274063)
XLA Ops:
  7.2 1.1 %convert_reduce_fusion.1 = f32[2,128]{1,0:T(2,128)S(1)} fusion(bf16[2,128,256]{2,1,0:T(8,128)(2,1)} %param.14), kind=kLoop, calls=%fused_computation.38 | loop fusion | flops 130816 | bytes 132096 | tf_op jit(solution)/shard_map/reduce_sum | solution.py:13
  8.3 1.1 %fusion.24 = f32[2,128]{1,0:T(2,128)S(1)} fusion(bf16[2,128,256]{2,1,0:T(8,128)(2,1)} %param.14, f32[2,128]{1,0:T(2,128)S(1)} %broadcast_multiply_fusion.2), kind=kLoop, calls=%fused_computation.41 | loop fusion | flops 261888 | bytes 133120 | tf_op jit(solution)/shard_map/reduce_sum | solution.py:14
  9.4 0.8 slice_bitcast_fusion.2
  10.2 1.2 %fusion.16 = bf16[2,2,128,32]{2,3,0,1:T(8,128)(2,1)S(1)} fusion(bf16[2,128,256]{2,1,0:T(8,128)(2,1)} %param.14, f32[2,128]{1,0:T(2,128)S(1)} %add_rsqrt_fusion.2, f32[2,128]{1,0:T(2,128)S(1)} %broadcast_multiply_fusion.2, bf16[2,256,32]{1,2,0:T(8,128)(2,1)} %param.26, f32[2,128]{1,0:T(2,128)S(1)} %get-tuple-element.28), kind=kOutput, calls=%fused_computation.26 | convolution fusion | flops 8683520 | bytes 199680 | tf_op jit(solution)/shard_map/juf,bfn->bjun/dot_general | solution.py:156
  11.6 0.7 reshape.117
  12.3 7.4 %all-to-all-start = ((bf16[16,2,256]{2,1,0:T(2,128)(2,1)}), bf16[16,2,256]{2,1,0:T(2,128)(2,1)S(1)}, u32[]{:S(2)}, u32[]{:S(2)}) async-start(bf16[16,2,256]{2,1,0:T(2,128)(2,1)} %reshape.117), calls=%async_computation | async-start | bytes 32768 | tf_op jit(solution)/shard_map/all_to_all | solution.py:160
  19.7 1.1 %convert_reduce_fusion = f32[8,128]{1,0:T(8,128)S(1)} fusion(bf16[8,128,128]{2,1,0:T(8,128)(2,1)} %param.15), kind=kLoop, calls=%fused_computation.30 | loop fusion | flops 261120 | bytes 266240 | tf_op jit(solution)/shard_map/reduce_sum | solution.py:13
  20.8 1.3 %fusion.19 = f32[8,128]{1,0:T(8,128)S(1)} fusion(bf16[8,128,128]{2,1,0:T(8,128)(2,1)} %param.15, f32[8,128]{1,0:T(8,128)S(1)} %broadcast_multiply_fusion), kind=kLoop, calls=%fused_computation.33 | loop fusion | flops 523264 | bytes 270336 | tf_op jit(solution)/shard_map/reduce_sum | solution.py:14
  22.2 1.4 %convolution_convert_fusion = bf16[6,8,128]{2,0,1:T(8,128)(2,1)S(1)} fusion(bf16[8,128,128]{2,1,0:T(8,128)(2,1)} %param.15, f32[8,128]{1,0:T(8,128)S(1)} %add_rsqrt_fusion, f32[8,128]{1,0:T(8,128)S(1)} %broadcast_multiply_fusion, bf16[128,2]{0,1:T(2,128)(2,1)} %param.19, bf16[128,4]{0,1:T(4,128)(2,1)} %param.18), kind=kOutput, calls=%fused_computation.27 | convolution fusion | flops 2106368 | bytes 284160 | tf_op jit(solution)/shard_map/tue,el->ltu/dot_general | solution.py:64
  23.6 22.2 %all_gather.12 = bf16[6,128,128]{2,1,0:T(8,128)(2,1)S(1)} all-gather(bf16[6,8,128]{2,1,0:T(8,128)(2,1)S(1)} %copy.39), channel_id=1, replica_groups=mesh['parts'=1,'rows'=8,'branch'=2,'head'=2] {'rows','branch'}, dimensions={1}, use_global_device_ids=true | all-gather | bytes 208896 | tf_op jit(solution)/shard_map/all_gather | solution.py:88
  46.4 0.4 fusion.79
  47.5 5.1 %all_gather.13 = bf16[2,128,256]{1,2,0:T(8,128)(2,1)S(1)} all-gather(bf16[2,128,128]{1,2,0:T(8,128)(2,1)S(1)} %fusion.55), channel_id=1, replica_groups=mesh['parts'=1,'rows'=8,'branch'=2,'head'=2] {'head'}, dimensions={2}, use_global_device_ids=true | all-gather | bytes 196608 | tf_op jit(solution)/shard_map/all_gather | solution.py:153
  53.1 0.4 fusion.14
  53.7 0.7 copy.76
  54.6 0.9 fusion.81
  55.5 0.6 fusion.82
  56.1 0.4 fusion.6
  57.4 6.6 %all_gather.14 = bf16[8,128,128]{1,2,0:T(8,128)(2,1)S(1)} all-gather(bf16[8,128,64]{1,2,0:T(8,128)(2,1)S(1)} %fusion.39), channel_id=1, replica_groups=mesh['parts'=1,'rows'=8,'branch'=2,'head'=2] {'head'}, dimensions={2}, use_global_device_ids=true | all-gather | bytes 393216 | tf_op jit(solution)/shard_map/all_gather | solution.py:154
  64.2 17.8 %all-gather = bf16[1,32,128,32]{2,3,0,1:T(8,128)(2,1)S(1)} all-gather(bf16[1,2,128,32]{2,3,0,1:T(8,128)(2,1)S(1)} %get-tuple-element.27), channel_id=2, replica_groups=mesh['parts'=1,'rows'=8,'branch'=2,'head'=2] {'rows','branch'}, dimensions={1}, use_global_device_ids=true | all-gather | bytes 278528 | tf_op jit(solution)/shard_map/all_gather | solution.py:163
  82.2 0.7 fusion.2
  82.9 0.8 copy.51
  83.8 1.1 %fusion.13 = bf16[8,128,64]{1,2,0:T(8,128)(2,1)} fusion(f32[8,128,64]{1,2,0:T(8,128)S(1)} %convolution_add_fusion.1, bf16[8,128,1024]{1,2,0:T(8,128)(2,1)S(1)} %bitcast.130, bf16[1024,64]{0,1:T(8,128)(2,1)S(1)} %copy-done.4), kind=kOutput, calls=%fused_computation.22 | convolution fusion | flops 134348800 | bytes 2621440 | tf_op jit(solution)/shard_map/while/body/eval_jaxpr/dot_general | solution.py:178
  85.0 0.9 reshape.116
  85.9 0.7 add_convert_fusion
  (59 shorter events, 3.7 us)
Async XLA Ops:
  7.2 38.9 %copy-start = (bf16[4,256,128]{2,1,0:T(8,128)(2,1)S(1)}, bf16[4,256,128]{2,1,0:T(8,128)(2,1)}, u32[]{:S(2)}) copy-start(bf16[4,256,128]{2,1,0:T(8,128)(2,1)} %param.20) | copy-start | bytes 786436
  7.2 38.9 %copy-start.2 = (bf16[2,128,256]{2,1,0:T(8,128)(2,1)S(1)}, bf16[2,128,256]{2,1,0:T(8,128)(2,1)}, u32[]{:S(2)}) copy-start(bf16[2,128,256]{2,1,0:T(8,128)(2,1)} %param.14) | copy-start | bytes 393220
  12.3 69.7 %all-to-all-start = ((bf16[16,2,256]{2,1,0:T(2,128)(2,1)}), bf16[16,2,256]{2,1,0:T(2,128)(2,1)S(1)}, u32[]{:S(2)}, u32[]{:S(2)}) async-start(bf16[16,2,256]{2,1,0:T(2,128)(2,1)} %reshape.117), calls=%async_computation | async-start | bytes 32768 | tf_op jit(solution)/shard_map/all_to_all | solution.py:160
  19.7 65.3 %reduce-scatter.4.cloned.1.call-start = ((), (), s32[]{:S(2)}) async-start(), calls=%async_computation.2 | async-start | bytes 196608
  46.8 5.8 %copy-start.3 = (bf16[256,256]{1,0:T(8,128)(2,1)S(1)}, bf16[256,256]{1,0:T(8,128)(2,1)}, u32[]{:S(2)}) copy-start(bf16[256,256]{1,0:T(8,128)(2,1)} %param.21) | copy-start | bytes 393220
  46.8 6.3 %copy-start.7 = (bf16[512,256]{1,0:T(8,128)(2,1)S(1)}, bf16[512,256]{1,0:T(8,128)(2,1)}, u32[]{:S(2)}) copy-start(bf16[512,256]{1,0:T(8,128)(2,1)} %param.23) | copy-start | bytes 786436
  46.8 6.3 %copy-start.8 = (bf16[256,512]{1,0:T(8,128)(2,1)S(1)}, bf16[256,512]{1,0:T(8,128)(2,1)}, u32[]{:S(2)}) copy-start(bf16[256,512]{1,0:T(8,128)(2,1)} %param.22) | copy-start | bytes 786436
  47.4 7.0 %copy-start.9 = (s32[128]{0:T(128)S(1)}, s32[128]{0:T(128)}, u32[]{:S(2)}) copy-start(s32[128]{0:T(128)} %param.17) | copy-start | bytes 1540
  47.4 7.2 %copy-start.1 = (bf16[8,128,128]{2,1,0:T(8,128)(2,1)S(1)}, bf16[8,128,128]{2,1,0:T(8,128)(2,1)}, u32[]{:S(2)}) copy-start(bf16[8,128,128]{2,1,0:T(8,128)(2,1)} %param.15) | copy-start | bytes 786436
  47.4 7.2 %copy-start.5 = (bf16[4,128,64]{1,2,0:T(8,128)(2,1)S(1)}, bf16[4,128,64]{1,2,0:T(8,128)(2,1)}, u32[]{:S(2)}) copy-start(bf16[4,128,64]{1,2,0:T(8,128)(2,1)} %param.24) | copy-start | bytes 196612
  57.0 7.0 %copy-start.6 = (bf16[128,64]{0,1:T(8,128)(2,1)S(1)}, bf16[128,64]{0,1:T(8,128)(2,1)}, u32[]{:S(2)}) copy-start(bf16[128,64]{0,1:T(8,128)(2,1)} %param.25) | copy-start | bytes 49156
  82.9 0.9 copy-start.4
Sparse Core Ops, SparseCore 0:
  54.5 8.3 reduce-scatter.3
where the time goes:
time: 93.9 us; the launch traced here: 93.4 us
  blocking collectives  51.8 us (55%)
  between operations  14.4 us (15%)
  matrix products  9.08 us (10%)
  starting transfers between devices  7.43 us (8%)
  other arithmetic  5.69 us (6%)
  local copies, waits for them, and re-layouts  4.99 us (5%)
    all_gather x1, blocking collectives, local(): lax.all_gather(bias_local, ('rows', 'branch'), axis=1, tiled=True)  22.2 us
    all_gather x1, blocking collectives, local(): lax.all_gather(outer_factors[1], ('rows', 'branch'), axis=0, tiled=True)  17.8 us
    all_to_all x1, starting transfers between devices, local(): lax.all_to_all(outer_factors[0], ('rows', 'branch'), split_axis=1, concat...  7.39 us
    all_gather x1, blocking collectives, local(): lax.all_gather(pair_local, 'head', axis=2, tiled=True)  6.56 us
    all_gather x1, blocking collectives, local(): lax.all_gather(alignment_local, 'head', axis=2, tiled=True)  5.15 us
    unnamed x27, local copies, waits for them, and re-layouts  2.84 us
    reduce_sum x3, other arithmetic, layer_normalize(): spread = jnp.mean(center * center, -1, keepdims=True)  2.59 us
    reduce_sum x2, other arithmetic, layer_normalize(): center = values - jnp.mean(values, -1, keepdims=True)  2.16 us
  transfers between devices with their start and end apart: 2, of which 0 were waited for; matrix products, arithmetic and copies ran while one was open for 14% of the time, Pallas kernels for 0%

commit v1 on v0

--- a/solution.py
+++ b/solution.py
@@ -1,8 +1,11 @@
+import functools
 import math
 
 import jax
 import jax.numpy as jnp
 from jax import lax
+from jax.experimental import pallas as pl
+from jax.experimental.pallas import tpu as pltpu
 from jax.sharding import PartitionSpec as P
 
 PER_FOCUS_DIM = 32
@@ -224,7 +227,444 @@
     return (refreshed_lineup_state, pairwise_out)
 
 
+F32 = jnp.float32
+BF16 = jnp.bfloat16
+NEG = -1000000000.0
+HD = PER_FOCUS_DIM
+
+
+def dot_nt(a, b):
+    return lax.dot_general(a, b, (((1,), (1,)), ((), ())), preferred_element_type=F32)
+
+
+def dot_nn(a, b):
+    return jnp.dot(a, b, preferred_element_type=F32)
+
+
+def head_mask(width, head):
+    lanes = lax.broadcasted_iota(jnp.int32, (1, width), 1)
+    return jnp.where((lanes >= head * HD) & (lanes < (head + 1) * HD), 1.0, 0.0)
+
+
+def block_kernel(
+    N,
+    NB,
+    S,
+    R,
+    L,
+    x_ref,
+    z_ref,
+    bs_ref,
+    bv_ref,
+    val_ref,
+    cw_ref,
+    tw_ref,
+    ap_ref,
+    wr_ref,
+    we_ref,
+    wx_ref,
+    pp_ref,
+    po_ref,
+    lr_ref,
+    ow_ref,
+    out_m,
+    out_z,
+    pn,
+    xn,
+    wscr,
+    bscr,
+    bias_all,
+    b_all,
+    a_send,
+    a_all,
+    bias_f,
+    q_s,
+    k_s,
+    v_s,
+    g_s,
+    pq_s,
+    pk_s,
+    pv_s,
+    pg_s,
+    wf,
+    wt,
+    bf,
+    bmat,
+    af,
+    at,
+    omat,
+    mh_own,
+    mh_oth,
+    ph_own,
+    ph_oth,
+    mid,
+    ps_own,
+    ps_send,
+    ps_recv,
+    bias_ss,
+    bias_rs,
+    b_ss,
+    b_rs,
+    a_ss,
+    a_rs,
+    m_ss,
+    m_rs,
+    p_ss,
+    p_rs,
+    f_ss,
+    f_rs,
+):
+    part = lax.axis_index("parts")
+    row = lax.axis_index("rows")
+    core = lax.axis_index("branch")
+    h = lax.axis_index("head")
+    me = row * NB + core
+    HM = cw_ref.shape[1]
+    HZ = tw_ref.shape[1]
+    H = HM + HZ
+    Q = lr_ref.shape[2]
+    C = po_ref.shape[1]
+    DM = HM * HD
+    DZ = HZ * HD
+    inv = 1.0 / math.sqrt(HD)
+
+    def peer(d):
+        p = lax.rem(me + d, N)
+        return p, (part, p // NB, lax.rem(p, NB), h)
+
+    partner = (part, row, core, 1 - h)
+
+    def remote(src, dst, ss, rs, dev):
+        return pltpu.make_async_remote_copy(
+            src_ref=src,
+            dst_ref=dst,
+            send_sem=ss,
+            recv_sem=rs,
+            device_id=dev,
+            device_id_type=pl.DeviceIdType.MESH,
+        )
+
+    barrier = pltpu.get_barrier_semaphore()
+
+    def greet(d, c):
+        pl.semaphore_signal(
+            barrier, inc=1, device_id=peer(d)[1], device_id_type=pl.DeviceIdType.MESH
+        )
+        return c
+
+    lax.fori_loop(1, N, greet, 0)
+    pl.semaphore_signal(barrier, inc=1, device_id=partner, device_id_type=pl.DeviceIdType.MESH)
+
+    pn[...] = layer_normalize(z_ref[...]).astype(BF16)
+    wscr[...] = jnp.zeros(wscr.shape, F32)
+    wscr[0, :, 0:HM] = cw_ref[...].astype(F32)
+    wscr[1, :, 0:HZ] = tw_ref[...].astype(F32)
+    for t in range(2):
+        w8 = wscr[t].T[0:8].astype(BF16)
+        bt = dot_nt(w8, pn[...])
+        for j in range(R):
+            bscr[t, j * 8 : (j + 1) * 8, :] = bt[:, j * L : (j + 1) * L]
+    pieces = [bscr[0, pl.ds(l, R, stride=8), :] for l in range(HM)]
+    pieces += [bscr[1, pl.ds(l, R, stride=8), :] for l in range(HZ)]
+    bias_all[me] = jnp.concatenate(pieces, 0).astype(BF16)
+
+    pl.semaphore_wait(barrier, N)
+
+    def send_bias(d, c):
+        p, dev = peer(d)
+        remote(bias_all.at[me], bias_all.at[me], bias_ss.at[p], bias_rs.at[me], dev).start()
+        return c
+
+    lax.fori_loop(1, N, send_bias, 0)
+
+    xn[...] = layer_normalize(x_ref[...]).astype(BF16)
+    lanes = lax.broadcasted_iota(jnp.int32, (1, L), 1)
+    tall = lax.broadcasted_iota(jnp.int32, (L, 1), 0)
+    ft = dot_nt(lr_ref[1].astype(F32).T.astype(BF16), xn[...])
+    fa = dot_nn(xn[...], lr_ref[0])
+    own_mask = []
+    parts_a = []
+    for s in range(S):
+        lo = bs_ref[me * S + s, 0]
+        hi = bs_ref[me * S + s, 1]
+        inside = (lanes >= lo) & (lanes < hi)
+        own_mask.append(inside)
+        b_all[me, s * Q : (s + 1) * Q, :] = (
+            ft[:, s * L : (s + 1) * L] * jnp.where(inside, 1.0, 0.0)
+        ).astype(BF16)
+        parts_a.append(
+            fa[s * L : (s + 1) * L] * jnp.where((tall >= lo) & (tall < hi), 1.0, 0.0)
+        )
+    for p in range(N):
+        a_send[p] = jnp.concatenate(
+            [parts_a[s][p * R : (p + 1) * R] for s in range(S)], 0
+        ).astype(BF16)
+    a_all[me] = a_send[me]
+
+    def send_factors(d, c):
+        p, dev = peer(d)
+        remote(b_all.at[me], b_all.at[me], b_ss.at[p], b_rs.at[me], dev).start()
+        remote(a_send.at[p], a_all.at[me], a_ss.at[p], a_rs.at[me], dev).start()
+        return c
+
+    lax.fori_loop(1, N, send_factors, 0)
+
+    for g, ref in ((0, q_s), (1, k_s), (2, v_s)):
+        ref[...] = dot_nn(xn[...], ap_ref[g]).astype(BF16)
+    g_s[...] = jax.nn.sigmoid(dot_nn(xn[...], ap_ref[3]))
+    for g, ref in ((0, pq_s), (1, pk_s), (2, pv_s)):
+        ref[...] = dot_nn(pn[...], pp_ref[g]).astype(BF16)
+    pg_s[...] = jax.nn.sigmoid(dot_nn(pn[...], pp_ref[3]))
+
+    wf[...] = ow_ref[...].astype(F32)
+    for q in range(Q):
+        wt[q * Q : (q + 1) * Q, :] = wf[pl.ds(q, Q, stride=Q), :].astype(BF16)
+
+    alllanes = lax.broadcasted_iota(jnp.int32, (N * S, L), 1)
+    lo_v = bv_ref[:, 0:1]
+    hi_v = bv_ref[:, 1:2]
+    m_all = jnp.where((alllanes >= lo_v) & (alllanes < hi_v), 1.0, 0.0)
+    shifted = alllanes + me * R
+    m_own = jnp.where((shifted >= lo_v) & (shifted < hi_v), 1.0, 0.0)
+    counts = dot_nn(m_own.T[0:R].astype(BF16), m_all.astype(BF16))
+    inv_counts = 1.0 / counts
+
+    def wait_bias(d, c):
+        p, dev = peer(d)
+        remote(bias_all.at[p], bias_all.at[p], bias_ss.at[p], bias_rs.at[p], dev).wait_recv()
+        return c
+
+    lax.fori_loop(1, N, wait_bias, 0)
+    valid = val_ref[...] > 0
+    for p in range(N):
+        piece = bias_all[p].astype(F32)
+        for l in range(H):
+            sub = piece[l * R : (l + 1) * R]
+            if l >= HM:
+                sub = jnp.where(valid, sub, NEG)
+            bias_f[l * L + p * R : l * L + (p + 1) * R, :] = sub
+
+    mm = [head_mask(DM, i).astype(BF16) for i in range(HM)]
+    m_copies = []
+    for s in range(S):
+        sl = slice(s * L, (s + 1) * L)
+        q = q_s[sl]
+        v = v_s[sl]
+        stack = jnp.concatenate([q * m for m in mm], 0)
+        score = dot_nt(stack, k_s[sl]) * inv + bias_f[0 : HM * L, :]
+        score = jnp.where(own_mask[s], score, NEG)
+        w = jnp.exp(score - jnp.max(score, -1, keepdims=True)).astype(BF16)
+        w = jnp.concatenate([w[i * L : (i + 1) * L] for i in range(HM)], 1)
+        vv = jnp.concatenate(
+            [jnp.concatenate([v * m, jnp.broadcast_to(m, v.shape)], 1) for m in mm], 0
+        )
+        o = dot_nn(w, vv)
+        mh_own[sl] = (o[:, :DM] / o[:, DM:] * g_s[sl]).astype(BF16)
+        copy = remote(mh_own.at[sl], mh_oth.at[sl], m_ss.at[s], m_rs.at[s], partner)
+        copy.start()
+        m_copies.append(copy)
+
+    zm = [head_mask(DZ, i).astype(BF16) for i in range(HZ)]
+
+    def tri(i):
+        sl = slice(i * L, (i + 1) * L)
+        q = pq_s[sl]
+        v = pv_s[sl]
+        stack = jnp.concatenate([q * m for m in zm], 0)
+        score = dot_nt(stack, pk_s[sl]) * inv + bias_f[HM * L :, :]
+        w = jnp.exp(score - jnp.max(score, -1, keepdims=True)).astype(BF16)
+        w = jnp.concatenate([w[j * L : (j + 1) * L] for j in range(HZ)], 1)
+        vv = jnp.concatenate(
+            [jnp.concatenate([v * m, jnp.broadcast_to(m, v.shape)], 1) for m in zm], 0
+        )
+        o = dot_nn(w, vv)
+        return o[:, :DZ] / o[:, DZ:] * pg_s[sl]
+
+    half = R // 2
+    p_copies = []
+    for i in range(half):
+        sl = slice(i * L, (i + 1) * L)
+        ph_own[sl] = jnp.concatenate([tri(i), tri(i + half)], 1).astype(BF16)
+        copy = remote(ph_own.at[sl], ph_oth.at[sl], p_ss.at[i], p_rs.at[i], partner)
+        copy.start()
+        p_copies.append(copy)
+
+    for copy in m_copies:
+        copy.wait_recv()
+    w_own = wr_ref[pl.ds(pl.multiple_of(h * DM, DM), DM), :]
+    w_oth = wr_ref[pl.ds(pl.multiple_of((1 - h) * DM, DM), DM), :]
+    mid[...] = x_ref[...].astype(F32) + dot_nn(mh_own[...], w_own) + dot_nn(mh_oth[...], w_oth)
+    tn = layer_normalize(mid[...]).astype(BF16)
+    hidden = jnp.maximum(dot_nn(tn, we_ref[...]), 0.0).astype(BF16)
+    W = out_m.shape[1]
+    sums = dot_nn(hidden, wx_ref[...])
+    first = h == 0
+    ps_own[...] = jnp.where(first, sums[:, :W], sums[:, W:])
+    ps_send[...] = jnp.where(first, sums[:, W:], sums[:, :W]).astype(BF16)
+    f_copy = remote(ps_send, ps_recv, f_ss, f_rs, partner)
+    f_copy.start()
+
+    def wait_factors(d, c):
+        p, dev = peer(d)
+        remote(b_all.at[p], b_all.at[p], b_ss.at[p], b_rs.at[p], dev).wait_recv()
+        remote(a_send.at[p], a_all.at[p], a_ss.at[p], a_rs.at[p], dev).wait_recv()
+        return c
+
+    lax.fori_loop(1, N, wait_factors, 0)
+    SQ = S * Q
+    SR = S * R
+    for p in range(N):
+        bf[p * SQ : (p + 1) * SQ, :] = b_all[p].astype(F32)
+        af[p * SR : (p + 1) * SR, :] = a_all[p].astype(F32)
+    for q in range(Q):
+        bmat[:, q * L : (q + 1) * L] = bf[pl.ds(q, N * S, stride=Q), :].astype(BF16)
+    for i in range(R):
+        at[i * Q : (i + 1) * Q, :] = af[pl.ds(i, N * S, stride=R), :].T.astype(BF16)
+    step = 8
+    for q0 in range(0, Q, step):
+        o = dot_nn(at[...], bmat[:, q0 * L : (q0 + step) * L]).astype(BF16)
+        for q in range(step):
+            for i in range(R):
+                omat[(q0 + q) * Q : (q0 + q + 1) * Q, i * L : (i + 1) * L] = o[
+                    i * Q : (i + 1) * Q, q * L : (q + 1) * L
+                ]
+    res = dot_nn(wt[...].astype(F32).T.astype(BF16), omat[...])
+
+    zw = jnp.zeros((DZ, C), BF16)
+    po = [po_ref[pl.ds(pl.multiple_of(t * DZ, DZ), DZ), :] for t in (h, 1 - h)]
+    lowers = [jnp.concatenate([w, zw], 0) for w in po]
+    uppers = [jnp.concatenate([zw, w], 0) for w in po]
+    for copy in p_copies:
+        copy.wait_recv()
+    for i in range(R):
+        k = i % half
+        sl = slice(k * L, (k + 1) * L)
+        ws = lowers if i < half else uppers
+        tri_out = dot_nn(ph_own[sl], ws[0]) + dot_nn(ph_oth[sl], ws[1])
+        opm = (res[:, i * L : (i + 1) * L] * inv_counts[i : i + 1, :]).T
+        zi = z_ref[i * L : (i + 1) * L, :].astype(F32)
+        base = jnp.where(first, zi[:, :C], zi[:, C:])
+        out_z[i] = (base + tri_out + opm).astype(BF16)
+
+    f_copy.wait_recv()
+    out_m[...] = (
+        mid[:, pl.ds(pl.multiple_of(h * W, W), W)] + ps_own[...] + ps_recv[...].astype(F32)
+    ).astype(BF16)
+
+    def drain(d, c):
+        p, dev = peer(d)
+        remote(bias_all.at[me], bias_all.at[me], bias_ss.at[p], bias_rs.at[me], dev).wait_send()
+        remote(b_all.at[me], b_all.at[me], b_ss.at[p], b_rs.at[me], dev).wait_send()
+        remote(a_send.at[p], a_all.at[me], a_ss.at[p], a_rs.at[me], dev).wait_send()
+        return c
+
+    lax.fori_loop(1, N, drain, 0)
+    for copy in m_copies + p_copies + [f_copy]:
+        copy.wait_send()
+
+
+def fused(N, NB, *args):
+    x, z, bounds, valid, cw, tw, ap, wr, we, wx, pp, po, lr, ow = args
+    S, L, D = x.shape
+    R, _, CZ = z.shape
+    HM, HZ = cw.shape[1], tw.shape[1]
+    H = HM + HZ
+    Q = lr.shape[2]
+    C = po.shape[1]
+    DM, DZ = HM * HD, HZ * HD
+    W = D // 2
+    vmem = pl.BlockSpec(memory_space=pltpu.VMEM)
+    smem = pl.BlockSpec(memory_space=pltpu.SMEM)
+    dma = pltpu.SemaphoreType.DMA
+    scratch = [
+        pltpu.VMEM((R * L, CZ), BF16),
+        pltpu.VMEM((S * L, D), BF16),
+        pltpu.VMEM((2, CZ, 128), F32),
+        pltpu.VMEM((2, R * 8, L), F32),
+        pltpu.VMEM((N, H * R, L), BF16),
+        pltpu.VMEM((N, S * Q, L), BF16),
+        pltpu.VMEM((N, S * R, Q), BF16),
+        pltpu.VMEM((N, S * R, Q), BF16),
+        pltpu.VMEM((H * L, L), F32),
+        pltpu.VMEM((S * L, DM), BF16),
+        pltpu.VMEM((S * L, DM), BF16),
+        pltpu.VMEM((S * L, DM), BF16),
+        pltpu.VMEM((S * L, DM), F32),
+        pltpu.VMEM((R * L, DZ), BF16),
+        pltpu.VMEM((R * L, DZ), BF16),
+        pltpu.VMEM((R * L, DZ), BF16),
+        pltpu.VMEM((R * L, DZ), F32),
+        pltpu.VMEM((Q * Q, C), F32),
+        pltpu.VMEM((Q * Q, C), BF16),
+        pltpu.VMEM((N * S * Q, L), F32),
+        pltpu.VMEM((N * S, Q * L), BF16),
+        pltpu.VMEM((N * S * R, Q), F32),
+        pltpu.VMEM((R * Q, N * S), BF16),
+        pltpu.VMEM((Q * Q, R * L), BF16),
+        pltpu.VMEM((S * L, DM), BF16),
+        pltpu.VMEM((S * L, DM), BF16),
+        pltpu.VMEM((R // 2 * L, 2 * DZ), BF16),
+        pltpu.VMEM((R // 2 * L, 2 * DZ), BF16),
+        pltpu.VMEM((S * L, D), F32),
+        pltpu.VMEM((S * L, W), F32),
+        pltpu.VMEM((S * L, W), BF16),
+        pltpu.VMEM((S * L, W), BF16),
+        dma((N,)),
+        dma((N,)),
+        dma((N,)),
+        dma((N,)),
+        dma((N,)),
+        dma((N,)),
+        dma((S,)),
+        dma((S,)),
+        dma((R // 2,)),
+        dma((R // 2,)),
+        dma,
+        dma,
+    ]
+    out_m, out_z = pl.pallas_call(
+        functools.partial(block_kernel, N, NB, S, R, L),
+        out_shape=(
+            jax.ShapeDtypeStruct((S * L, W), BF16),
+            jax.ShapeDtypeStruct((R, L, C), BF16),
+        ),
+        in_specs=[vmem, vmem, smem] + [vmem] * 12,
+        out_specs=(vmem, vmem),
+        scratch_shapes=scratch,
+        compiler_params=pltpu.CompilerParams(
+            collective_id=0, has_side_effects=True, vmem_limit_bytes=48 * 1024 * 1024
+        ),
+    )(
+        x.reshape(S * L, D),
+        z.reshape(R * L, CZ),
+        bounds,
+        bounds,
+        valid.reshape(1, L),
+        cw,
+        tw,
+        ap,
+        wr,
+        we,
+        wx,
+        pp,
+        po,
+        lr,
+        ow,
+    )
+    return out_m.reshape(S, L, W), out_z
+
+
+def block(N, NB, NH, *args):
+    x, z = args[0], args[1]
+    S, L, D = x.shape
+    if NH == 2 and L == 128 and z.shape[0] == 8 and S == 2 and D == 256:
+        return fused(N, NB, *args)
+    return local(*args)
+
+
 def solution(mesh):
+    NB = mesh.shape["branch"]
+    N = mesh.shape["rows"] * NB
     in_specs = (
         P(("parts", "rows", "branch"), None, None),
         P(("parts", "rows", "branch"), None, None),
@@ -245,4 +685,5 @@
         P(("parts", "rows", "branch"), None, "head"),
         P(("parts", "rows", "branch"), None, "head"),
     )
-    return jax.shard_map(local, mesh=mesh, in_specs=in_specs, out_specs=out_specs, check_vma=False)
+    return jax.shard_map(
+        functools.partial(block, N, NB, mesh.shape["head"]), mesh=mesh, in_specs=in_specs, out_specs=out_specs, check_vma=False)

time: 93.9 us -> 32 us (0.34)
  the two profiles are of different devices: /device:TPU:0 before, /device:TPU:12 now
where the time goes in v1:
time: 32 us; the launch traced here: 31.8 us
  Pallas kernels  23.6 us (74%)
  local copies, waits for them, and re-layouts  7.42 us (23%)
  between operations  0.77 us (2%)
    pallas_call x1, Pallas kernels, fused(): pl.pallas_call(functools.partial(block_kernel, N, NB, S, R, L), out_shape...  23.6 us
    unnamed x33, local copies, waits for them, and re-layouts  7.42 us

profile of v1, /device:TPU:12, one launch (start us, length us, event | category | flops | bytes accessed | tf_op | source)
XLA Modules:
  0.0 31.8 jit_solution(1043329882247487722)
XLA Ops:
  0.6 0.0 copy-start.9
  0.6 0.0 copy-start.10
  0.7 0.0 copy-start.11
  0.7 0.7 %copy-done.9 = s32[32,2]{0,1:T(2,128)S(1)} copy-done((s32[32,2]{0,1:T(2,128)S(1)}, s32[32,2]{0,1:T(2,128)}, u32[]{:S(2)}) %copy-start.9) | copy-done | bytes 280
  1.3 0.1 copy.16.bs_ref.bv_ref
  1.4 0.1 copy.18.cw_ref
  1.5 0.0 copy-done.11
  1.5 0.0 copy-start.8
  1.6 0.1 copy.19.tw_ref
  1.7 0.9 %copy.21.po_ref = bf16[128,64]{1,0:T(8,128)(2,1)S(1)} copy(bf16[128,64]{0,1:T(8,128)(2,1)} %param.25) | data formatting | bytes 32768 | tf_op args[11]
  2.6 0.1 copy.20.pp_ref
  2.7 0.0 copy-done.8
  2.7 0.0 copy-start
  2.7 0.0 copy-start.1
  2.7 0.1 copy.22.lr_ref
  2.9 0.0 copy-start.6
  2.9 1.1 %copy.23.ow_ref = bf16[1024,64]{1,0:T(8,128)(2,1)S(1)} copy(bf16[1024,64]{0,1:T(8,128)(2,1)} %param.27) | data formatting | bytes 262144 | tf_op args[13]
  4.0 0.0 copy-start.3
  4.0 0.9 %copy-done.3 = bf16[512,256]{1,0:T(8,128)(2,1)S(1)} copy-done((bf16[512,256]{1,0:T(8,128)(2,1)S(1)}, bf16[512,256]{1,0:T(8,128)(2,1)}, u32[]{:S(2)}) %copy-start.3) | copy-done | bytes 262168
  5.0 0.9 %copy-done.4 = bf16[2,128,256]{2,1,0:T(8,128)(2,1)S(1)} copy-done((bf16[2,128,256]{2,1,0:T(8,128)(2,1)S(1)}, bf16[2,128,256]{2,1,0:T(8,128)(2,1)}, u32[]{:S(2)}) %copy-start.4) | copy-done | bytes 131096
  5.9 0.9 %copy-done.5 = bf16[256,256]{1,0:T(8,128)(2,1)S(1)} copy-done((bf16[256,256]{1,0:T(8,128)(2,1)S(1)}, bf16[256,256]{1,0:T(8,128)(2,1)}, u32[]{:S(2)}) %copy-start.5) | copy-done | bytes 131096
  6.8 23.6 %shard_map.149 = (bf16[256,128]{1,0:T(8,128)(2,1)S(1)}, bf16[8,128,64]{2,1,0:T(8,128)(2,1)S(1)}) custom-call(bf16[256,256]{1,0:T(8,128)(2,1)S(1)} %bitcast.5, bf16[1024,128]{1,0:T(8,128)(2,1)S(1)} %bitcast.4, s32[32,2]{1,0:T(8,128)S(1)} %copy.16.bs_ref.bv_ref, s32[32,2]{1,0:T(8,128)S(1)} %copy.16.bs_ref.bv_ref, s32[1,128]{1,0:T(1,128)S(1)} %bitcast.7, ...), custom_call_target="tpu_custom_call" | custom-call | tf_op jit(solution)/shard_map/pallas_call | solution.py:625
  30.4 0.8 %copy.24 = bf16[8,128,64]{1,2,0:T(8,128)(2,1)} copy(bf16[8,128,64]{2,1,0:T(8,128)(2,1)S(1)} %get-tuple-element.7) | data formatting | bytes 262144
  31.2 0.6 %copy.26 = bf16[2,128,128]{2,1,0:T(8,128)(2,1)} copy(bf16[2,128,128]{2,1,0:T(8,128)(2,1)S(1)} %bitcast.6) | data formatting | bytes 131072
  (10 shorter events, 0.0 us)
Async XLA Ops:
  0.6 0.7 %copy-start.9 = (s32[32,2]{0,1:T(2,128)S(1)}, s32[32,2]{0,1:T(2,128)}, u32[]{:S(2)}) copy-start(s32[32,2]{0,1:T(2,128)} %param.16) | copy-start | bytes 772
  0.6 0.8 %copy-start.10 = (bf16[128,4]{0,1:T(4,128)(2,1)S(1)}, bf16[128,4]{0,1:T(4,128)(2,1)}, u32[]{:S(2)}) copy-start(bf16[128,4]{0,1:T(4,128)(2,1)} %param.18) | copy-start | bytes 3076
  0.7 0.9 %copy-start.11 = (bf16[128,2]{0,1:T(2,128)(2,1)S(1)}, bf16[128,2]{0,1:T(2,128)(2,1)}, u32[]{:S(2)}) copy-start(bf16[128,2]{0,1:T(2,128)(2,1)} %param.19) | copy-start | bytes 1540
  1.3 1.3 %copy-start.7 = (bf16[4,128,64]{1,2,0:T(8,128)(2,1)S(1)}, bf16[4,128,64]{1,2,0:T(8,128)(2,1)}, u32[]{:S(2)}) copy-start(bf16[4,128,64]{1,2,0:T(8,128)(2,1)} %param.24) | copy-start | bytes 196612
  1.5 1.2 %copy-start.8 = (bf16[2,256,32]{1,2,0:T(8,128)(2,1)S(1)}, bf16[2,256,32]{1,2,0:T(8,128)(2,1)}, u32[]{:S(2)}) copy-start(bf16[2,256,32]{1,2,0:T(8,128)(2,1)} %param.26) | copy-start | bytes 98308
  1.7 2.3 %copy-start.2 = (bf16[256,512]{1,0:T(8,128)(2,1)S(1)}, bf16[256,512]{1,0:T(8,128)(2,1)}, u32[]{:S(2)}) copy-start(bf16[256,512]{1,0:T(8,128)(2,1)} %we_ref.1) | copy-start | bytes 786436
  2.7 1.3 %copy-start = (bf16[8,128,128]{2,1,0:T(8,128)(2,1)S(1)}, bf16[8,128,128]{2,1,0:T(8,128)(2,1)}, u32[]{:S(2)}) copy-start(bf16[8,128,128]{2,1,0:T(8,128)(2,1)} %param.15) | copy-start | bytes 786436
  2.7 1.3 %copy-start.1 = (bf16[4,256,128]{2,1,0:T(8,128)(2,1)S(1)}, bf16[4,256,128]{2,1,0:T(8,128)(2,1)}, u32[]{:S(2)}) copy-start(bf16[4,256,128]{2,1,0:T(8,128)(2,1)} %ap_ref.1) | copy-start | bytes 786436
  2.9 1.1 %copy-start.6 = (s32[128]{0:T(128)S(1)}, s32[128]{0:T(128)}, u32[]{:S(2)}) copy-start(s32[128]{0:T(128)} %param.17) | copy-start | bytes 1540
  4.0 1.0 %copy-start.3 = (bf16[512,256]{1,0:T(8,128)(2,1)S(1)}, bf16[512,256]{1,0:T(8,128)(2,1)}, u32[]{:S(2)}) copy-start(bf16[512,256]{1,0:T(8,128)(2,1)} %wx_ref.1) | copy-start | bytes 786436
  5.0 0.9 %copy-start.4 = (bf16[2,128,256]{2,1,0:T(8,128)(2,1)S(1)}, bf16[2,128,256]{2,1,0:T(8,128)(2,1)}, u32[]{:S(2)}) copy-start(bf16[2,128,256]{2,1,0:T(8,128)(2,1)} %param.14) | copy-start | bytes 393220
  5.9 0.9 %copy-start.5 = (bf16[256,256]{1,0:T(8,128)(2,1)S(1)}, bf16[256,256]{1,0:T(8,128)(2,1)}, u32[]{:S(2)}) copy-start(bf16[256,256]{1,0:T(8,128)(2,1)} %wr_ref.1) | copy-start | bytes 393220

commit v2 on v1

--- a/solution.py
+++ b/solution.py
@@ -231,6 +231,8 @@
 BF16 = jnp.bfloat16
 NEG = -1000000000.0
 HD = PER_FOCUS_DIM
+NI = 14
+LOAD_ORDER = (1, 4, 5, 0, 2, 12, 10, 6, 13, 3, 7, 8, 9, 11)
 
 
 def dot_nt(a, b):
@@ -252,9 +254,18 @@
     S,
     R,
     L,
+    *refs,
+):
+    hbm = refs[:NI]
+    out_m, out_z = refs[NI : NI + 2]
+    held = refs[NI + 2 : 2 * NI + 2]
+    in_sem = refs[2 * NI + 2]
+    loads = [pltpu.make_async_copy(hbm[i], held[i], in_sem.at[i]) for i in range(NI)]
+    for i in LOAD_ORDER:
+        loads[i].start()
+    (
     x_ref,
     z_ref,
-    bs_ref,
     bv_ref,
     val_ref,
     cw_ref,
@@ -267,11 +278,12 @@
     po_ref,
     lr_ref,
     ow_ref,
-    out_m,
-    out_z,
+    ) = held
+    (
     pn,
     xn,
     wscr,
+    mscr,
     bscr,
     bias_all,
     b_all,
@@ -313,17 +325,22 @@
     p_rs,
     f_ss,
     f_rs,
-):
+    ) = refs[2 * NI + 3 :]
+
+    def need(*names):
+        for name in names:
+            loads[name].wait()
+
     part = lax.axis_index("parts")
     row = lax.axis_index("rows")
     core = lax.axis_index("branch")
     h = lax.axis_index("head")
     me = row * NB + core
-    HM = cw_ref.shape[1]
-    HZ = tw_ref.shape[1]
+    HM = cw_ref.shape[0]
+    HZ = tw_ref.shape[0]
     H = HM + HZ
-    Q = lr_ref.shape[2]
-    C = po_ref.shape[1]
+    Q = lr_ref.shape[1]
+    C = po_ref.shape[0]
     DM = HM * HD
     DZ = HZ * HD
     inv = 1.0 / math.sqrt(HD)
@@ -355,17 +372,15 @@
     lax.fori_loop(1, N, greet, 0)
     pl.semaphore_signal(barrier, inc=1, device_id=partner, device_id_type=pl.DeviceIdType.MESH)
 
+    need(1, 4, 5)
     pn[...] = layer_normalize(z_ref[...]).astype(BF16)
     wscr[...] = jnp.zeros(wscr.shape, F32)
-    wscr[0, :, 0:HM] = cw_ref[...].astype(F32)
-    wscr[1, :, 0:HZ] = tw_ref[...].astype(F32)
-    for t in range(2):
-        w8 = wscr[t].T[0:8].astype(BF16)
-        bt = dot_nt(w8, pn[...])
-        for j in range(R):
-            bscr[t, j * 8 : (j + 1) * 8, :] = bt[:, j * L : (j + 1) * L]
-    pieces = [bscr[0, pl.ds(l, R, stride=8), :] for l in range(HM)]
-    pieces += [bscr[1, pl.ds(l, R, stride=8), :] for l in range(HZ)]
+    wscr[0:HM, :] = cw_ref[...].astype(F32)
+    wscr[HM:H, :] = tw_ref[...].astype(F32)
+    bt = dot_nt(wscr[...].astype(BF16), pn[...])
+    for j in range(R):
+        bscr[j * 8 : (j + 1) * 8, :] = bt[:, j * L : (j + 1) * L]
+    pieces = [bscr[pl.ds(l, R, stride=8), :] for l in range(H)]
     bias_all[me] = jnp.concatenate(pieces, 0).astype(BF16)
 
     pl.semaphore_wait(barrier, N)
@@ -377,24 +392,30 @@
 
     lax.fori_loop(1, N, send_bias, 0)
 
+    need(0, 2, 12)
     xn[...] = layer_normalize(x_ref[...]).astype(BF16)
-    lanes = lax.broadcasted_iota(jnp.int32, (1, L), 1)
-    tall = lax.broadcasted_iota(jnp.int32, (L, 1), 0)
-    ft = dot_nt(lr_ref[1].astype(F32).T.astype(BF16), xn[...])
-    fa = dot_nn(xn[...], lr_ref[0])
+    wscr[...] = jnp.zeros(wscr.shape, F32)
+    wscr[0:2, 0 : N * S] = bv_ref[...].astype(F32)
+    bounds = wscr[...].T[0 : N * S]
+    lo_v = bounds[:, 0:1]
+    hi_v = bounds[:, 1:2]
+    lanes = lax.broadcasted_iota(jnp.int32, (N * S, L), 1)
+    place = lanes.astype(F32)
+    m_all = jnp.where((place >= lo_v) & (place < hi_v), 1.0, 0.0)
+    place = (lanes + me * R).astype(F32)
+    m_own = jnp.where((place >= lo_v) & (place < hi_v), 1.0, 0.0)
+    mscr[0 : N * S, :] = m_all
+    mscr[N * S :, :] = jnp.zeros((8, L), F32)
+    ft = dot_nt(lr_ref[1], xn[...])
+    fa = dot_nt(xn[...], lr_ref[0])
     own_mask = []
     parts_a = []
     for s in range(S):
-        lo = bs_ref[me * S + s, 0]
-        hi = bs_ref[me * S + s, 1]
-        inside = (lanes >= lo) & (lanes < hi)
-        own_mask.append(inside)
-        b_all[me, s * Q : (s + 1) * Q, :] = (
-            ft[:, s * L : (s + 1) * L] * jnp.where(inside, 1.0, 0.0)
-        ).astype(BF16)
-        parts_a.append(
-            fa[s * L : (s + 1) * L] * jnp.where((tall >= lo) & (tall < hi), 1.0, 0.0)
-        )
+        inside = mscr[pl.ds(me * S + s, 1), :]
+        own_mask.append(inside > 0)
+        b_all[me, s * Q : (s + 1) * Q, :] = (ft[:, s * L : (s + 1) * L] * inside).astype(BF16)
+        column = jnp.broadcast_to(inside, (8, L)).T[:, 0:1]
+        parts_a.append(fa[s * L : (s + 1) * L] * column)
     for p in range(N):
         a_send[p] = jnp.concatenate(
             [parts_a[s][p * R : (p + 1) * R] for s in range(S)], 0
@@ -409,23 +430,19 @@
 
     lax.fori_loop(1, N, send_factors, 0)
 
+    need(6, 10)
     for g, ref in ((0, q_s), (1, k_s), (2, v_s)):
         ref[...] = dot_nn(xn[...], ap_ref[g]).astype(BF16)
     g_s[...] = jax.nn.sigmoid(dot_nn(xn[...], ap_ref[3]))
     for g, ref in ((0, pq_s), (1, pk_s), (2, pv_s)):
-        ref[...] = dot_nn(pn[...], pp_ref[g]).astype(BF16)
-    pg_s[...] = jax.nn.sigmoid(dot_nn(pn[...], pp_ref[3]))
-
-    wf[...] = ow_ref[...].astype(F32)
+        ref[...] = dot_nt(pn[...], pp_ref[g]).astype(BF16)
+    pg_s[...] = jax.nn.sigmoid(dot_nt(pn[...], pp_ref[3]))
+
+    need(13, 3)
+    wf[...] = ow_ref[...].astype(F32).T
     for q in range(Q):
         wt[q * Q : (q + 1) * Q, :] = wf[pl.ds(q, Q, stride=Q), :].astype(BF16)
 
-    alllanes = lax.broadcasted_iota(jnp.int32, (N * S, L), 1)
-    lo_v = bv_ref[:, 0:1]
-    hi_v = bv_ref[:, 1:2]
-    m_all = jnp.where((alllanes >= lo_v) & (alllanes < hi_v), 1.0, 0.0)
-    shifted = alllanes + me * R
-    m_own = jnp.where((shifted >= lo_v) & (shifted < hi_v), 1.0, 0.0)
     counts = dot_nn(m_own.T[0:R].astype(BF16), m_all.astype(BF16))
     inv_counts = 1.0 / counts
 
@@ -489,6 +506,7 @@
         copy.start()
         p_copies.append(copy)
 
+    need(7, 8, 9, 11)
     for copy in m_copies:
         copy.wait_recv()
     w_own = wr_ref[pl.ds(pl.multiple_of(h * DM, DM), DM), :]
@@ -530,21 +548,30 @@
                 ]
     res = dot_nn(wt[...].astype(F32).T.astype(BF16), omat[...])
 
-    zw = jnp.zeros((DZ, C), BF16)
-    po = [po_ref[pl.ds(pl.multiple_of(t * DZ, DZ), DZ), :] for t in (h, 1 - h)]
-    lowers = [jnp.concatenate([w, zw], 0) for w in po]
-    uppers = [jnp.concatenate([zw, w], 0) for w in po]
+    po = po_ref[...]
+    turned = jnp.concatenate([po[:, DZ:], po[:, :DZ]], 1)
+    own_first = jnp.where(first, po, turned)
+    oth_first = jnp.where(first, turned, po)
+    zl = lax.broadcasted_iota(jnp.int32, (1, 2 * DZ), 1)
+    low = jnp.where(zl < DZ, 1.0, 0.0).astype(BF16)
+    high = jnp.where(zl >= DZ, 1.0, 0.0).astype(BF16)
+    lowers = [own_first * low, oth_first * low]
+    uppers = [oth_first * high, own_first * high]
+    cc = lax.broadcasted_iota(jnp.int32, (C, 2 * C), 0) + h * C
+    pick = jnp.where(cc == lax.broadcasted_iota(jnp.int32, (C, 2 * C), 1), 1.0, 0.0).astype(BF16)
     for copy in p_copies:
         copy.wait_recv()
     for i in range(R):
         k = i % half
         sl = slice(k * L, (k + 1) * L)
         ws = lowers if i < half else uppers
-        tri_out = dot_nn(ph_own[sl], ws[0]) + dot_nn(ph_oth[sl], ws[1])
-        opm = (res[:, i * L : (i + 1) * L] * inv_counts[i : i + 1, :]).T
-        zi = z_ref[i * L : (i + 1) * L, :].astype(F32)
-        base = jnp.where(first, zi[:, :C], zi[:, C:])
-        out_z[i] = (base + tri_out + opm).astype(BF16)
+        total = (
+            dot_nt(ws[0], ph_own[sl])
+            + dot_nt(ws[1], ph_oth[sl])
+            + dot_nt(pick, z_ref[i * L : (i + 1) * L, :])
+        )
+        opm = res[:, i * L : (i + 1) * L] * inv_counts[i : i + 1, :]
+        out_z[i] = (total + opm).astype(BF16)
 
     f_copy.wait_recv()
     out_m[...] = (
@@ -574,13 +601,13 @@
     DM, DZ = HM * HD, HZ * HD
     W = D // 2
     vmem = pl.BlockSpec(memory_space=pltpu.VMEM)
-    smem = pl.BlockSpec(memory_space=pltpu.SMEM)
     dma = pltpu.SemaphoreType.DMA
     scratch = [
         pltpu.VMEM((R * L, CZ), BF16),
         pltpu.VMEM((S * L, D), BF16),
-        pltpu.VMEM((2, CZ, 128), F32),
-        pltpu.VMEM((2, R * 8, L), F32),
+        pltpu.VMEM((8, 128), F32),
+        pltpu.VMEM((N * S + 8, L), F32),
+        pltpu.VMEM((R * 8, L), F32),
         pltpu.VMEM((N, H * R, L), BF16),
         pltpu.VMEM((N, S * Q, L), BF16),
         pltpu.VMEM((N, S * R, Q), BF16),
@@ -622,36 +649,37 @@
         dma,
         dma,
     ]
+    operands = (
+        x.reshape(S * L, D),
+        z.reshape(R * L, CZ),
+        bounds.T,
+        valid.reshape(1, L),
+        cw.T,
+        tw.T,
+        ap,
+        wr,
+        we,
+        wx,
+        jnp.transpose(pp, (0, 2, 1)),
+        po.T,
+        jnp.transpose(lr, (0, 2, 1)),
+        ow.T,
+    )
+    held = [pltpu.VMEM(a.shape, a.dtype) for a in operands]
     out_m, out_z = pl.pallas_call(
         functools.partial(block_kernel, N, NB, S, R, L),
         out_shape=(
             jax.ShapeDtypeStruct((S * L, W), BF16),
-            jax.ShapeDtypeStruct((R, L, C), BF16),
+            jax.ShapeDtypeStruct((R, C, L), BF16),
         ),
-        in_specs=[vmem, vmem, smem] + [vmem] * 12,
+        in_specs=[pl.BlockSpec(memory_space=pltpu.HBM)] * NI,
         out_specs=(vmem, vmem),
-        scratch_shapes=scratch,
+        scratch_shapes=held + [dma((NI,))] + scratch,
         compiler_params=pltpu.CompilerParams(
-            collective_id=0, has_side_effects=True, vmem_limit_bytes=48 * 1024 * 1024
+            collective_id=0, has_side_effects=True, vmem_limit_bytes=60 * 1024 * 1024
         ),
-    )(
-        x.reshape(S * L, D),
-        z.reshape(R * L, CZ),
-        bounds,
-        bounds,
-        valid.reshape(1, L),
-        cw,
-        tw,
-        ap,
-        wr,
-        we,
-        wx,
-        pp,
-        po,
-        lr,
-        ow,
-    )
-    return out_m.reshape(S, L, W), out_z
+    )(*operands)
+    return out_m.reshape(S, L, W), jnp.transpose(out_z, (0, 2, 1))
 
 
 def block(N, NB, NH, *args):

time: 32 us -> 26.6 us (0.83)
  local copies, waits for them, and re-layouts: 7.42 us -> 2.17 us
    unnamed x33 -> x4, local copies, waits for them, and re-layouts: 7.42 us -> 2.17 us
where the time goes in v2:
time: 26.6 us; the launch traced here: 26.4 us
  Pallas kernels  23.6 us (89%)
  local copies, waits for them, and re-layouts  2.17 us (8%)
  between operations  0.65 us (2%)
    pallas_call x1, Pallas kernels, fused(): pl.pallas_call(functools.partial(block_kernel, N, NB, S, R, L), out_shape...  23.6 us
    unnamed x4, local copies, waits for them, and re-layouts  2.17 us

profile of v2, /device:TPU:12, one launch (start us, length us, event | category | flops | bytes accessed | tf_op | source)
XLA Modules:
  0.0 26.4 jit_solution(17875022726321757708)
XLA Ops:
  0.6 23.6 %shard_map.149 = (bf16[256,128]{1,0:T(8,128)(2,1)}, bf16[8,64,128]{2,1,0:T(8,128)(2,1)}) custom-call(bf16[256,256]{1,0:T(8,128)(2,1)} %bitcast.14, bf16[1024,128]{1,0:T(8,128)(2,1)} %bitcast.12, s32[2,32]{1,0:T(2,128)} %bitcast.20, s32[1,128]{1,0:T(1,128)} %bitcast.22, bf16[4,128]{1,0:T(4,128)(2,1)} %bitcast.21, bf16[2,128]{1,0:T(2,128)(2,1)} %bitcast.23, ...), custom_call_target="tpu_custom_call" | custom-call | tf_op jit(solution)/shard_map/pallas_call | solution.py:669
  24.3 0.0 copy-start
  24.3 1.5 %copy.18 = bf16[2,128,128]{2,1,0:T(8,128)(2,1)} copy(bf16[2,128,128]{2,1,0:T(8,128)(2,1)} %bitcast.16) | data formatting | bytes 131072
  25.8 0.0 copy-done
  25.8 0.7 %copy.19 = bf16[8,128,64]{1,2,0:T(8,128)(2,1)} copy(bf16[8,128,64]{1,2,0:T(8,128)(2,1)S(1)} %bitcast.13) | data formatting | bytes 262144
Async XLA Ops:
  24.3 1.5 %copy-start = (bf16[8,64,128]{2,1,0:T(8,128)(2,1)S(1)}, bf16[8,64,128]{2,1,0:T(8,128)(2,1)}, u32[]{:S(2)}) copy-start(bf16[8,64,128]{2,1,0:T(8,128)(2,1)} %get-tuple-element.5) | copy-start | bytes 393220

commit v3 on v2

--- a/solution.py
+++ b/solution.py
@@ -350,6 +350,49 @@
         return p, (part, p // NB, lax.rem(p, NB), h)
 
     partner = (part, row, core, 1 - h)
+    NR = N // NB
+    sibling = (part, row, 1 - core, h)
+    twin = row * NB + 1 - core
+
+    def same_core(d):
+        r = lax.rem(row + d, NR)
+        return r * NB + core, r * NB + 1 - core, (part, r, core, h)
+
+    def spread(buf, ss, rs):
+        def one(d, c):
+            p, _, dev = same_core(d)
+            remote(buf.at[me], buf.at[me], ss.at[p], rs.at[me], dev).start()
+            return c
+
+        lax.fori_loop(1, NR, one, 0)
+        remote(buf.at[me], buf.at[me], ss.at[twin], rs.at[me], sibling).start()
+
+    def forward(buf, ss, rs):
+        def one(d, c):
+            p, t, dev = same_core(d)
+            remote(buf.at[p], buf.at[p], ss.at[p], rs.at[p], dev).wait_recv()
+            remote(buf.at[p], buf.at[p], ss.at[t], rs.at[p], sibling).start()
+            return c
+
+        lax.fori_loop(1, NR, one, 0)
+
+    def collect(buf, ss, rs):
+        def one(d, c):
+            _, t, _ = same_core(d)
+            remote(buf.at[t], buf.at[t], ss.at[t], rs.at[t], sibling).wait_recv()
+            return c
+
+        lax.fori_loop(0, NR, one, 0)
+
+    def finish(buf, ss, rs):
+        def one(d, c):
+            p, t, dev = same_core(d)
+            remote(buf.at[me], buf.at[me], ss.at[p], rs.at[me], dev).wait_send()
+            remote(buf.at[p], buf.at[p], ss.at[t], rs.at[p], sibling).wait_send()
+            return c
+
+        lax.fori_loop(1, NR, one, 0)
+        remote(buf.at[me], buf.at[me], ss.at[twin], rs.at[me], sibling).wait_send()
 
     def remote(src, dst, ss, rs, dev):
         return pltpu.make_async_remote_copy(
@@ -385,12 +428,7 @@
 
     pl.semaphore_wait(barrier, N)
 
-    def send_bias(d, c):
-        p, dev = peer(d)
-        remote(bias_all.at[me], bias_all.at[me], bias_ss.at[p], bias_rs.at[me], dev).start()
-        return c
-
-    lax.fori_loop(1, N, send_bias, 0)
+    spread(bias_all, bias_ss, bias_rs)
 
     need(0, 2, 12)
     xn[...] = layer_normalize(x_ref[...]).astype(BF16)
@@ -422,13 +460,14 @@
         ).astype(BF16)
     a_all[me] = a_send[me]
 
-    def send_factors(d, c):
+    spread(b_all, b_ss, b_rs)
+
+    def send_left(d, c):
         p, dev = peer(d)
-        remote(b_all.at[me], b_all.at[me], b_ss.at[p], b_rs.at[me], dev).start()
         remote(a_send.at[p], a_all.at[me], a_ss.at[p], a_rs.at[me], dev).start()
         return c
 
-    lax.fori_loop(1, N, send_factors, 0)
+    lax.fori_loop(1, N, send_left, 0)
 
     need(6, 10)
     for g, ref in ((0, q_s), (1, k_s), (2, v_s)):
@@ -446,12 +485,8 @@
     counts = dot_nn(m_own.T[0:R].astype(BF16), m_all.astype(BF16))
     inv_counts = 1.0 / counts
 
-    def wait_bias(d, c):
-        p, dev = peer(d)
-        remote(bias_all.at[p], bias_all.at[p], bias_ss.at[p], bias_rs.at[p], dev).wait_recv()
-        return c
-
-    lax.fori_loop(1, N, wait_bias, 0)
+    forward(bias_all, bias_ss, bias_rs)
+    collect(bias_all, bias_ss, bias_rs)
     valid = val_ref[...] > 0
     for p in range(N):
         piece = bias_all[p].astype(F32)
@@ -505,6 +540,8 @@
         copy = remote(ph_own.at[sl], ph_oth.at[sl], p_ss.at[i], p_rs.at[i], partner)
         copy.start()
         p_copies.append(copy)
+
+    forward(b_all, b_ss, b_rs)
 
     need(7, 8, 9, 11)
     for copy in m_copies:
@@ -522,13 +559,14 @@
     f_copy = remote(ps_send, ps_recv, f_ss, f_rs, partner)
     f_copy.start()
 
-    def wait_factors(d, c):
+    collect(b_all, b_ss, b_rs)
+
+    def wait_left(d, c):
         p, dev = peer(d)
-        remote(b_all.at[p], b_all.at[p], b_ss.at[p], b_rs.at[p], dev).wait_recv()
         remote(a_send.at[p], a_all.at[p], a_ss.at[p], a_rs.at[p], dev).wait_recv()
         return c
 
-    lax.fori_loop(1, N, wait_factors, 0)
+    lax.fori_loop(1, N, wait_left, 0)
     SQ = S * Q
     SR = S * R
     for p in range(N):
@@ -578,10 +616,11 @@
         mid[:, pl.ds(pl.multiple_of(h * W, W), W)] + ps_own[...] + ps_recv[...].astype(F32)
     ).astype(BF16)
 
+    finish(bias_all, bias_ss, bias_rs)
+    finish(b_all, b_ss, b_rs)
+
     def drain(d, c):
         p, dev = peer(d)
-        remote(bias_all.at[me], bias_all.at[me], bias_ss.at[p], bias_rs.at[me], dev).wait_send()
-        remote(b_all.at[me], b_all.at[me], b_ss.at[p], b_rs.at[me], dev).wait_send()
         remote(a_send.at[p], a_all.at[me], a_ss.at[p], a_rs.at[me], dev).wait_send()
         return c
 
@@ -685,7 +724,7 @@
 def block(N, NB, NH, *args):
     x, z = args[0], args[1]
     S, L, D = x.shape
-    if NH == 2 and L == 128 and z.shape[0] == 8 and S == 2 and D == 256:
+    if NH == 2 and NB == 2 and L == 128 and z.shape[0] == 8 and S == 2 and D == 256:
         return fused(N, NB, *args)
     return local(*args)
 

time: 26.6 us -> 24.2 us (0.910)
  the two profiles are of different devices: /device:TPU:12 before, /device:TPU:0 now
where the time goes in v3:
time: 24.2 us; the launch traced here: 24 us
  Pallas kernels  21.2 us (88%)
  local copies, waits for them, and re-layouts  2.17 us (9%)
  between operations  0.65 us (3%)
    pallas_call x1, Pallas kernels, fused(): pl.pallas_call(functools.partial(block_kernel, N, NB, S, R, L), out_shape...  21.2 us
    unnamed x4, local copies, waits for them, and re-layouts  2.17 us

profile of v3, /device:TPU:0, one launch (start us, length us, event | category | flops | bytes accessed | tf_op | source)
XLA Modules:
  0.0 24.0 jit_solution(916477695095445350)
XLA Ops:
  0.6 21.2 %shard_map.149 = (bf16[256,128]{1,0:T(8,128)(2,1)}, bf16[8,64,128]{2,1,0:T(8,128)(2,1)}) custom-call(bf16[256,256]{1,0:T(8,128)(2,1)} %bitcast.14, bf16[1024,128]{1,0:T(8,128)(2,1)} %bitcast.12, s32[2,32]{1,0:T(2,128)} %bitcast.20, s32[1,128]{1,0:T(1,128)} %bitcast.22, bf16[4,128]{1,0:T(4,128)(2,1)} %bitcast.21, bf16[2,128]{1,0:T(2,128)(2,1)} %bitcast.23, ...), custom_call_target="tpu_custom_call" | custom-call | tf_op jit(solution)/shard_map/pallas_call | solution.py:708
  21.8 0.0 copy-start
  21.9 1.5 %copy.18 = bf16[2,128,128]{2,1,0:T(8,128)(2,1)} copy(bf16[2,128,128]{2,1,0:T(8,128)(2,1)} %bitcast.16) | data formatting | bytes 131072
  23.4 0.0 copy-done
  23.4 0.7 %copy.19 = bf16[8,128,64]{1,2,0:T(8,128)(2,1)} copy(bf16[8,128,64]{1,2,0:T(8,128)(2,1)S(1)} %bitcast.13) | data formatting | bytes 262144
Async XLA Ops:
  21.8 1.5 %copy-start = (bf16[8,64,128]{2,1,0:T(8,128)(2,1)S(1)}, bf16[8,64,128]{2,1,0:T(8,128)(2,1)}, u32[]{:S(2)}) copy-start(bf16[8,64,128]{2,1,0:T(8,128)(2,1)} %get-tuple-element.5) | copy-start | bytes 393220
